TPU v7x, 256 devices: a whole 4x4x8 slice. The times are simulated.
256 devices in a mesh: sec: 4 (over x_lo, core), dev: 64 (over x_hi, z, y).
Axes of the slice: x: 4 (x_hi: 2, x_lo: 2; x = x_hi * 2 + x_lo), y: 4, z: 8, core: 2. Of those that a mesh axis runs over, the one named last changes fastest.
Arguments:
- queries: bfloat16 [256, 128, 576], P(('sec', 'dev')), may hold values from -56 to 56
- latent_cache: bfloat16 [256, 4096, 576], P(('sec', 'dev')), may hold values from -4 to 4
- cache_lengths: int32 [256], P(('sec', 'dev')), may hold values from 512 to 4096, as said below
- stream: bfloat16 [512, 7168], P('dev'), may hold values from -6 to 6
- norm_gain: float32 [7168], replicated, may hold values from 0.1 to 1.9
- expert_ids: int32 [512, 8], P('dev'), may hold values from 0 to 15, all different within a row; in each aligned block of 8 rows (0 to 7, 8 to 15, ...) at most 5 rows name the same one
- route_weights: float32 [512, 8], P('dev'), may hold values from 0.1 to 1
- w_gate: bfloat16 [64, 7168, 512], P('dev', None, 'sec'), may hold values from -0.0625 to 0.0625
- w_up: bfloat16 [64, 7168, 512], P('dev', None, 'sec'), may hold values from -0.0625 to 0.0625
- w_down: bfloat16 [64, 512, 7168], P('dev', 'sec'), may hold values from -0.125 to 0.125
Outputs:
- context: bfloat16 [256, 128, 512], P(('sec', 'dev'))
- mixed: bfloat16 [512, 7168], P('dev')
Inputs may be any that keep to these rules, and one draw needn't show every extreme that they name: `expert_ids`: each row names 8 distinct experts; within the 8 rows of one group no expert is named more than 5 times, a bound that some block reaches. `cache_lengths`: the longest sequence holds 4096 positions.
All inputs are finite; a program needn't handle non-finite values.
Results may differ from a plain program's by a relative error of at most 0.015.
Values may be sent and summed in bfloat16 or wider, within the bound.
No kernel may reach another device: no remote copies, remote signals or barrier semaphores. Data moves between devices by JAX's collectives and lax.ppermute only.
A program may use at most 128 MiB of HBM per device.

v0:
```python
import jax
import jax.numpy as jnp
from jax import lax
from jax.sharding import PartitionSpec as P

MOE_HIDDEN = 2048
LATENT = 512
HID_DEV = 128
score_scale = 192.0 ** (-0.5)


def slot_table(choices, count, capacity):
    experts = jnp.arange(count, dtype=jnp.int32)
    hit_count = jnp.sum((choices[..., None] == experts).astype(jnp.float32), axis=2)
    before = jnp.cumsum(hit_count, axis=1) - hit_count
    slot_ids = jnp.arange(capacity).astype(jnp.float32)
    picked = hit_count[..., None] * (before[..., None] == slot_ids).astype(jnp.float32)
    return (jnp.transpose(picked, (0, 2, 3, 1)), hit_count)


def local(
    queries,
    latent_cache,
    cache_lengths,
    stream,
    norm_gain,
    expert_ids,
    route_weights,
    w_gate,
    w_up,
    w_down,
):
    scores = (
        jnp.einsum("shk,slk->shl", queries, latent_cache, preferred_element_type=jnp.float32)
        * score_scale
    )
    visible = (
        jnp.arange(latent_cache.shape[1], dtype=jnp.int32)[None, None, :]
        < cache_lengths[:, None, None]
    )
    scores = jnp.where(visible, scores, jnp.float32(-1e30))
    peak = jnp.max(scores, axis=2, keepdims=True)
    powered = jnp.exp(scores - peak)
    probs = (powered / jnp.sum(powered, axis=2, keepdims=True)).astype(jnp.bfloat16)
    context = jnp.einsum(
        "shl,slk->shk", probs, latent_cache[:, :, :LATENT], preferred_element_type=jnp.float32
    ).astype(jnp.bfloat16)
    dev_count = lax.axis_size("dev")
    sec_count = lax.axis_size("sec")
    group_size = MOE_HIDDEN // (HID_DEV * sec_count)
    expert_count = dev_count // group_size
    row_count = stream.shape[0]
    top_count = expert_ids.shape[1]
    capacity = max(2, row_count * top_count * 5 // (4 * expert_count))
    width = stream.shape[1]
    stream_f = stream.astype(jnp.float32)
    scale_rows = lax.rsqrt(jnp.mean(stream_f * stream_f, axis=1, keepdims=True) + 1e-06)
    normed = (stream_f * scale_rows * norm_gain).astype(jnp.bfloat16)
    own_table, hit_count = slot_table(expert_ids[None], expert_count, capacity)
    own_table = own_table[0]
    all_rows, all_ids = (
        lax.all_gather(normed, "dev", axis=0, tiled=True),
        lax.all_gather(expert_ids, "dev", axis=0, tiled=True),
    )
    own_expert = lax.axis_index("dev") // group_size
    grouped_ids = all_ids.reshape(dev_count, row_count, top_count)
    named = jnp.sum((grouped_ids == own_expert).astype(jnp.float32), axis=2)
    before = jnp.cumsum(named, axis=1) - named
    slot_ids = jnp.arange(capacity).astype(jnp.float32)
    picked = named[:, None, :] * (before[:, None, :] == slot_ids[None, :, None]).astype(jnp.float32)
    received = jnp.einsum(
        "gjr,grd->gjd",
        picked.astype(jnp.bfloat16),
        all_rows.reshape(dev_count, row_count, width),
        preferred_element_type=jnp.float32,
    ).astype(jnp.bfloat16)
    slot_flat = received.reshape(dev_count * capacity, width)
    gate_proj = jnp.dot(slot_flat, w_gate[0], preferred_element_type=jnp.float32)
    up_proj = jnp.dot(slot_flat, w_up[0], preferred_element_type=jnp.float32)
    hidden = (jax.nn.silu(gate_proj) * up_proj).astype(jnp.bfloat16)
    partial_value = jnp.dot(hidden, w_down[0], preferred_element_type=jnp.float32).astype(
        jnp.bfloat16
    )
    experts = jnp.arange(expert_count, dtype=jnp.int32)
    weight_table = jnp.sum(
        route_weights[..., None] * (expert_ids[..., None] == experts).astype(jnp.float32), axis=1
    )
    weighted = own_table * jnp.transpose(weight_table)[:, None, :]
    returned = lax.all_to_all(
        partial_value.reshape(dev_count, capacity, width),
        "dev",
        split_axis=0,
        concat_axis=0,
        tiled=True,
    )
    block_sums = jnp.sum(
        returned.reshape(expert_count, group_size, capacity, width), axis=1, dtype=jnp.float32
    )
    section_part = jnp.einsum("ejr,ejd->rd", weighted, block_sums, precision=lax.Precision.HIGHEST)
    section_total = lax.psum(section_part.astype(jnp.bfloat16), "sec").astype(jnp.float32)
    mixed = (stream_f + section_total).astype(jnp.bfloat16)
    return (context, mixed)


def solution(mesh):
    return jax.shard_map(
        local,
        mesh=mesh,
        in_specs=(
            P(("sec", "dev"), None, None),
            P(("sec", "dev"), None, None),
            P(("sec", "dev")),
            P("dev", None),
            P(),
            P("dev", None),
            P("dev", None),
            P("dev", None, "sec"),
            P("dev", None, "sec"),
            P("dev", "sec", None),
        ),
        out_specs=(P(("sec", "dev"), None, None), P("dev", None)),
        check_vma=False,
    )
```

profile of v0, /device:TPU:1, one launch (start us, length us, event | category | flops | bytes accessed | tf_op | source)
XLA Modules:
  0.0 435.7 jit_solution(7749568602587736564)
XLA Ops:
  7.2 0.0 copy-start
  7.2 0.0 all-gather.2.cloned.1.call-start
  7.2 1.2 fusion.30
  8.4 1.6 fusion.32
  10.1 0.0 all-gather.2.cloned.1.call-update
  10.1 160.0 %all_gather.6 = s32[512,8]{1,0:T(8,128)S(1)} all-gather(s32[8,8]{1,0:T(8,128)} %param.15), channel_id=1, replica_groups=mesh['sec'=4,'dev'=64] {'dev'}, dimensions={0}, use_global_device_ids=true | all-gather | bytes 16640 | tf_op jit(solution)/shard_map/all_gather | solution.py:63
  170.1 0.1 convert_reduce_fusion.1
  170.3 0.1 reduce_window_sum.25
  170.4 0.2 reduce_window_sum.26
  170.6 0.0 all-gather.2.cloned.1.call-done
  170.6 8.2 %convolution_convert_fusion = bf16[64,5,7168]{2,1,0:T(8,128)(2,1)} fusion(bf16[512,7168]{1,0:T(8,128)(2,1)} %all-gather.2.cloned.1.call-done, f32[64,8]{1,0:T(8,128)S(1)} %reduce_window_sum.25, f32[64,8]{1,0:T(8,128)S(1)} %sub.33, f32[5]{0:T(128)S(1)} %iota_convert_fusion), kind=kOutput, calls=%fused_computation.1 | convolution fusion | flops 38999040 | bytes 11931668 | tf_op jit(solution)/shard_map/gjr,grd->gjd/dot_general | solution.py:71
  178.7 8.2 %reshape.143 = bf16[320,7168]{1,0:T(8,128)(2,1)} reshape(bf16[64,5,7168]{2,1,0:T(8,128)(2,1)} %convolution_convert_fusion) | data formatting | bytes 9175040 | tf_op jit(solution)/shard_map/reshape | solution.py:77
  187.0 4.2 fusion.12
  191.2 0.0 copy-done
  191.2 9.9 %convolution_convert_fusion.1 = bf16[320,7168]{1,0:T(8,128)(2,1)} fusion(bf16[1,128,7168]{2,1,0:T(8,128)(2,1)S(1)} %copy-done, bf16[320,7168]{1,0:T(8,128)(2,1)} %reshape.143, bf16[1,7168,128]{2,1,0:T(8,128)(2,1)} %param.18, f32[320,128]{1,0:T(8,128)S(1)} %fusion.12), kind=kOutput, calls=%fused_computation.2 | convolution fusion | flops 1176944640 | bytes 13008896 | tf_op jit(solution)/shard_map/dot_general | solution.py:81
  201.1 8.0 %reshape.144 = bf16[64,5,7168]{2,1,0:T(8,128)(2,1)} reshape(bf16[320,7168]{1,0:T(8,128)(2,1)} %convolution_convert_fusion.1) | data formatting | bytes 9175040 | tf_op jit(solution)/shard_map/reshape | solution.py:90
  209.1 5.9 %all-to-all-start = ((bf16[64,5,7168]{2,1,0:T(8,128)(2,1)}), bf16[64,5,7168]{2,1,0:T(8,128)(2,1)}, u32[]{:S(2)}, u32[]{:S(2)}) async-start(bf16[64,5,7168]{2,1,0:T(8,128)(2,1)} %reshape.144), calls=%async_computation | async-start | bytes 14680064 | tf_op jit(solution)/shard_map/all_to_all | solution.py:89
  215.0 0.2 all-reduce.2.cloned.1.call-start
  215.2 0.1 convert_reduce_fusion.2
  216.0 0.1 select_reduce_fusion
  216.1 0.0 copy-done.3
  216.1 3.5 fusion.55
  219.6 1.3 copy-done.1
  220.9 0.4 fusion.8
  221.3 126.4 %all-to-all-done = bf16[64,5,7168]{2,1,0:T(8,128)(2,1)} async-done(((bf16[64,5,7168]{2,1,0:T(8,128)(2,1)}), bf16[64,5,7168]{2,1,0:T(8,128)(2,1)}, u32[]{:S(2)}, u32[]{:S(2)}) %all-to-all-start) | async-done | bytes 4587552 | tf_op jit(solution)/shard_map/all_to_all | solution.py:89
  347.7 5.4 %convert_reduce_fusion = f32[16,5,7168]{2,1,0:T(8,128)S(1)} fusion(bf16[64,5,7168]{2,1,0:T(8,128)(2,1)} %all-to-all-done), kind=kLoop, calls=%fused_computation | loop fusion | flops 4014080 | bytes 6881280 | tf_op jit(solution)/shard_map/reduce_sum | solution.py:96
  353.1 4.2 fusion
  357.3 0.0 all-reduce.2.cloned.1.call-update
  357.4 0.0 copy-start.2
  357.4 5.1 %fusion.20 = bf16[1,128,512]{2,1,0:T(8,128)(2,1)} fusion(bf16[1,4096,576]{1,2,0:T(8,128)(2,1)} %param.11, f32[128,4096]{1,0:T(8,128)} %copy-done.1, f32[128]{0:T(128)S(1)} %fusion.8, f32[128]{0:T(128)S(1)} %get-tuple-element.2), kind=kOutput, calls=%fused_computation.23 | convolution fusion | flops 538509312 | bytes 6423552 | tf_op jit(solution)/shard_map/shl,slk->shk/dot_general | solution.py:45
  362.4 64.9 %all-reduce.2.cloned.1.call-done = bf16[8,7168]{1,0:T(8,128)(2,1)} async-done(((bf16[8,7168]{1,0:T(8,128)(2,1)}), bf16[8,7168]{1,0:T(8,128)(2,1)}) %all-reduce.2.cloned.1.call-update) | async-done | bytes 114704 | tf_op jit(solution)/shard_map/psum | solution.py:100
  427.3 1.6 fusion.33
  (13 shorter events, 0.1 us)
Async XLA Ops:
  7.2 184.0 %copy-start = (bf16[1,128,7168]{2,1,0:T(8,128)(2,1)S(1)}, bf16[1,128,7168]{2,1,0:T(8,128)(2,1)}, u32[]{:S(2)}) copy-start(bf16[1,128,7168]{2,1,0:T(8,128)(2,1)} %param.19) | copy-start | bytes 5505028
  7.2 163.4 %all-gather.2.cloned.1.call-start = ((), (), s32[]{:S(2)}) async-start(), calls=%async_computation.1 | async-start | bytes 7454720 | tf_op jit(solution)/shard_map/all_gather | solution.py:62
  209.1 6.1 %copy-start.4 = (s32[8,8]{1,0:T(8,128)S(1)}, s32[8,8]{1,0:T(8,128)}, u32[]{:S(2)}) copy-start(s32[8,8]{1,0:T(8,128)} %param.15) | copy-start | bytes 772
  209.1 6.9 %copy-start.5 = (f32[8,8]{1,0:T(8,128)S(1)}, f32[8,8]{1,0:T(8,128)}, u32[]{:S(2)}) copy-start(f32[8,8]{1,0:T(8,128)} %param.16) | copy-start | bytes 772
  209.1 7.0 %copy-start.3 = (bf16[1,128,576]{1,2,0:T(8,128)(2,1)S(1)}, bf16[1,128,576]{1,2,0:T(8,128)(2,1)}, u32[]{:S(2)}) copy-start(bf16[1,128,576]{1,2,0:T(8,128)(2,1)} %param.10) | copy-start | bytes 442372
  209.1 138.6 %all-to-all-start = ((bf16[64,5,7168]{2,1,0:T(8,128)(2,1)}), bf16[64,5,7168]{2,1,0:T(8,128)(2,1)}, u32[]{:S(2)}, u32[]{:S(2)}) async-start(bf16[64,5,7168]{2,1,0:T(8,128)(2,1)} %reshape.144), calls=%async_computation | async-start | bytes 14680064 | tf_op jit(solution)/shard_map/all_to_all | solution.py:89
  215.0 212.3 %all-reduce.2.cloned.1.call-start = ((), (), s32[]{:S(2)}) async-start(), calls=%async_computation.2 | async-start | bytes 229376 | tf_op jit(solution)/shard_map/psum | solution.py:100
  219.6 1.3 copy-start.1
  357.4 69.9 %copy-start.2 = (bf16[8,7168]{1,0:T(8,128)(2,1)S(1)}, bf16[8,7168]{1,0:T(8,128)(2,1)}, u32[]{:S(2)}) copy-start(bf16[8,7168]{1,0:T(8,128)(2,1)} %param.13) | copy-start | bytes 344068
Sparse Core Ops, SparseCore 0:
  12.2 145.7 all-gather.1
  357.5 69.7 all-reduce.1
where the time goes:
time: 436 us
  waiting for transfers between devices  191 us (44%)
  blocking collectives  160 us (37%)
  matrix products  35 us (8%)
  local copies, waits for them, and re-layouts  17.6 us (4%)
  between operations  14.8 us (3%)
  other arithmetic  10.8 us (2%)
  starting transfers between devices  6.12 us (1%)
    all_gather x1, blocking collectives, local(): lax.all_gather(expert_ids, 'dev', axis=0, tiled=True)  160 us
    all_to_all x1, waiting for transfers between devices, local(): lax.all_to_all(partial_value.reshape(dev_count, capacity, width), 'dev',...  126 us
    psum x1, waiting for transfers between devices, local(): lax.psum(section_part.astype(jnp.bfloat16), 'sec').astype(jnp.float32)  64.9 us
    dot_general x1, matrix products, local(): jnp.dot(hidden, w_down[0], preferred_element_type=jnp.float32)  9.9 us
  transfers between devices with their start and end apart: 3, of which 2 were waited for; matrix products, arithmetic and copies ran while one was open for 2% of the time, Pallas kernels for 0%

commit v1 on v0

--- a/solution.py
+++ b/solution.py
@@ -7,6 +7,11 @@
 LATENT = 512
 HID_DEV = 128
 score_scale = 192.0 ** (-0.5)
+
+
+def add_all(x, name):
+    parts = lax.all_gather(x, name)
+    return jnp.sum(parts, axis=0)
 
 
 def slot_table(choices, count, capacity):
@@ -97,7 +102,7 @@
         returned.reshape(expert_count, group_size, capacity, width), axis=1, dtype=jnp.float32
     )
     section_part = jnp.einsum("ejr,ejd->rd", weighted, block_sums, precision=lax.Precision.HIGHEST)
-    section_total = lax.psum(section_part.astype(jnp.bfloat16), "sec").astype(jnp.float32)
+    section_total = add_all(section_part.astype(jnp.bfloat16), "sec").astype(jnp.float32)
     mixed = (stream_f + section_total).astype(jnp.bfloat16)
     return (context, mixed)
 

time: 436 us -> 403 us (0.924)
  waiting for transfers between devices: 191 us -> 123 us
  blocking collectives: 160 us -> 197 us
    psum x1 -> x0, waiting for transfers between devices: 64.9 us -> none  [local(): lax.psum(section_part.astype(jnp.bfloat16), 'sec').astype(jnp.float32)]
    all_gather x0 -> x1, blocking collectives: none -> 37.4 us  [add_all(): parts = lax.all_gather(x, name)]
  transfers between devices with their start and end apart: 3 -> 2, of which waited for: 2 -> 1; matrix products, arithmetic and copies ran while one was open for 2% -> 2% of each run, Pallas kernels for 0% -> 0%
where the time goes in v1:
time: 403 us; the launch traced here: 402 us
  blocking collectives  197 us (49%)
  waiting for transfers between devices  123 us (31%)
  matrix products  33.7 us (8%)
  local copies, waits for them, and re-layouts  16.3 us (4%)
  between operations  14.8 us (4%)
  other arithmetic  9.93 us (2%)
  starting transfers between devices  6.08 us (2%)
    all_gather x1, blocking collectives, local(): lax.all_gather(expert_ids, 'dev', axis=0, tiled=True)  160 us
    all_to_all x1, waiting for transfers between devices, local(): lax.all_to_all(partial_value.reshape(dev_count, capacity, width), 'dev',...  123 us
    all_gather x1, blocking collectives, add_all(): parts = lax.all_gather(x, name)  37.4 us
    dot_general x1, matrix products, local(): jnp.dot(hidden, w_down[0], preferred_element_type=jnp.float32)  9.9 us
    reshape x1, local copies, waits for them, and re-layouts, local(): slot_flat = received.reshape(dev_count * capacity, width)  8.22 us
    dot_general x1, matrix products, local(): jnp.einsum('gjr,grd->gjd', picked.astype(jnp.bfloat16), all_rows.reshape(...  8.17 us
  transfers between devices with their start and end apart: 2, of which 1 were waited for; matrix products, arithmetic and copies ran while one was open for 2% of the time, Pallas kernels for 0%

profile of v1, /device:TPU:1, one launch (start us, length us, event | category | flops | bytes accessed | tf_op | source)
XLA Modules:
  0.0 401.7 jit_solution(2059073587830426192)
XLA Ops:
  7.2 0.0 copy-start
  7.2 0.0 all-gather.3.cloned.1.call-start
  7.2 1.2 fusion.30
  8.4 1.6 fusion.32
  10.1 0.0 all-gather.3.cloned.1.call-update
  10.1 160.0 %all_gather.12 = s32[512,8]{1,0:T(8,128)S(1)} all-gather(s32[8,8]{1,0:T(8,128)} %param.15), channel_id=1, replica_groups=mesh['sec'=4,'dev'=64] {'dev'}, dimensions={0}, use_global_device_ids=true | all-gather | bytes 16640 | tf_op jit(solution)/shard_map/all_gather | solution.py:68
  170.1 0.1 convert_reduce_fusion.1
  170.3 0.1 reduce_window_sum.25
  170.4 0.2 reduce_window_sum.26
  170.6 0.0 all-gather.3.cloned.1.call-done
  170.6 8.2 %convolution_convert_fusion = bf16[64,5,7168]{2,1,0:T(8,128)(2,1)} fusion(bf16[512,7168]{1,0:T(8,128)(2,1)} %all-gather.3.cloned.1.call-done, f32[64,8]{1,0:T(8,128)S(1)} %reduce_window_sum.25, f32[64,8]{1,0:T(8,128)S(1)} %sub.33, f32[5]{0:T(128)S(1)} %iota_convert_fusion), kind=kOutput, calls=%fused_computation.1 | convolution fusion | flops 38999040 | bytes 11931668 | tf_op jit(solution)/shard_map/gjr,grd->gjd/dot_general | solution.py:76
  178.7 8.2 %reshape.143 = bf16[320,7168]{1,0:T(8,128)(2,1)} reshape(bf16[64,5,7168]{2,1,0:T(8,128)(2,1)} %convolution_convert_fusion) | data formatting | bytes 9175040 | tf_op jit(solution)/shard_map/reshape | solution.py:82
  187.0 4.2 %fusion.12 = f32[320,128]{1,0:T(8,128)S(1)} fusion(bf16[320,7168]{1,0:T(8,128)(2,1)} %reshape.143, bf16[1,7168,128]{2,1,0:T(8,128)(2,1)} %param.17), kind=kOutput, calls=%fused_computation.19 | convolution fusion | flops 587202560 | bytes 6586368 | tf_op jit(solution)/shard_map/dot_general | solution.py:83
  191.2 0.0 copy-done
  191.2 9.9 %convolution_convert_fusion.1 = bf16[320,7168]{1,0:T(8,128)(2,1)} fusion(bf16[1,128,7168]{2,1,0:T(8,128)(2,1)S(1)} %copy-done, bf16[320,7168]{1,0:T(8,128)(2,1)} %reshape.143, bf16[1,7168,128]{2,1,0:T(8,128)(2,1)} %param.18, f32[320,128]{1,0:T(8,128)S(1)} %fusion.12), kind=kOutput, calls=%fused_computation.2 | convolution fusion | flops 1176944640 | bytes 13008896 | tf_op jit(solution)/shard_map/dot_general | solution.py:86
  201.1 8.0 %reshape.144 = bf16[64,5,7168]{2,1,0:T(8,128)(2,1)} reshape(bf16[320,7168]{1,0:T(8,128)(2,1)} %convolution_convert_fusion.1) | data formatting | bytes 9175040 | tf_op jit(solution)/shard_map/reshape | solution.py:95
  209.1 6.0 %all-to-all-start = ((bf16[64,5,7168]{2,1,0:T(8,128)(2,1)}), bf16[64,5,7168]{2,1,0:T(8,128)(2,1)}, u32[]{:S(2)}, u32[]{:S(2)}) async-start(bf16[64,5,7168]{2,1,0:T(8,128)(2,1)} %reshape.144), calls=%async_computation | async-start | bytes 14680064 | tf_op jit(solution)/shard_map/all_to_all | solution.py:94
  215.1 0.0 copy-done.3
  215.2 0.1 convert_reduce_fusion.2
  215.9 0.0 copy-done.4
  216.0 0.1 select_reduce_fusion
  216.1 0.0 copy-done.2
  216.1 3.5 fusion.55
  219.5 0.4 fusion.8
  220.0 4.4 %fusion.20 = bf16[1,128,512]{2,1,0:T(8,128)(2,1)} fusion(bf16[1,4096,576]{1,2,0:T(8,128)(2,1)} %param.11, f32[128,4096]{1,0:T(8,128)S(1)} %get-tuple-element.3, f32[128]{0:T(128)S(1)} %fusion.8, f32[128]{0:T(128)S(1)} %get-tuple-element.2), kind=kOutput, calls=%fused_computation.23 | convolution fusion | flops 538509312 | bytes 6423552 | tf_op jit(solution)/shard_map/shl,slk->shk/dot_general | solution.py:50
  224.4 123.4 %all-to-all-done = bf16[64,5,7168]{2,1,0:T(8,128)(2,1)} async-done(((bf16[64,5,7168]{2,1,0:T(8,128)(2,1)}), bf16[64,5,7168]{2,1,0:T(8,128)(2,1)}, u32[]{:S(2)}, u32[]{:S(2)}) %all-to-all-start) | async-done | bytes 4587552 | tf_op jit(solution)/shard_map/all_to_all | solution.py:94
  347.7 5.4 %convert_reduce_fusion = f32[16,5,7168]{2,1,0:T(8,128)S(1)} fusion(bf16[64,5,7168]{2,1,0:T(8,128)(2,1)} %all-to-all-done), kind=kLoop, calls=%fused_computation | loop fusion | flops 4014080 | bytes 6881280 | tf_op jit(solution)/shard_map/reduce_sum | solution.py:101
  353.1 3.6 fusion
  356.7 37.4 %all-gather = bf16[32,7168]{1,0:T(8,128)(2,1)S(1)} all-gather(bf16[8,7168]{1,0:T(8,128)(2,1)S(1)} %fusion), channel_id=2, replica_groups=mesh['sec'=4,'dev'=64] {'sec'}, dimensions={0}, use_global_device_ids=true | all-gather | bytes 573440 | tf_op jit(solution)/shard_map/all_gather | solution.py:13
  394.1 0.1 bitcast_reduce_fusion
  394.2 0.0 copy-done.1
  394.2 0.7 fusion.33
  (10 shorter events, 0.1 us)
Async XLA Ops:
  7.2 184.0 %copy-start = (bf16[1,128,7168]{2,1,0:T(8,128)(2,1)S(1)}, bf16[1,128,7168]{2,1,0:T(8,128)(2,1)}, u32[]{:S(2)}) copy-start(bf16[1,128,7168]{2,1,0:T(8,128)(2,1)} %param.19) | copy-start | bytes 5505028
  7.2 163.4 %all-gather.3.cloned.1.call-start = ((), (), s32[]{:S(2)}) async-start(), calls=%async_computation.1 | async-start | bytes 7454720 | tf_op jit(solution)/shard_map/all_gather | solution.py:67
  209.1 6.1 %copy-start.3 = (s32[8,8]{1,0:T(8,128)S(1)}, s32[8,8]{1,0:T(8,128)}, u32[]{:S(2)}) copy-start(s32[8,8]{1,0:T(8,128)} %param.15) | copy-start | bytes 772
  209.1 6.9 %copy-start.4 = (f32[8,8]{1,0:T(8,128)S(1)}, f32[8,8]{1,0:T(8,128)}, u32[]{:S(2)}) copy-start(f32[8,8]{1,0:T(8,128)} %param.16) | copy-start | bytes 772
  209.1 7.0 %copy-start.2 = (bf16[1,128,576]{1,2,0:T(8,128)(2,1)S(1)}, bf16[1,128,576]{1,2,0:T(8,128)(2,1)}, u32[]{:S(2)}) copy-start(bf16[1,128,576]{1,2,0:T(8,128)(2,1)} %param.10) | copy-start | bytes 442372
  209.1 138.6 %all-to-all-start = ((bf16[64,5,7168]{2,1,0:T(8,128)(2,1)}), bf16[64,5,7168]{2,1,0:T(8,128)(2,1)}, u32[]{:S(2)}, u32[]{:S(2)}) async-start(bf16[64,5,7168]{2,1,0:T(8,128)(2,1)} %reshape.144), calls=%async_computation | async-start | bytes 14680064 | tf_op jit(solution)/shard_map/all_to_all | solution.py:94
  224.4 169.8 %copy-start.1 = (bf16[8,7168]{1,0:T(8,128)(2,1)S(1)}, bf16[8,7168]{1,0:T(8,128)(2,1)}, u32[]{:S(2)}) copy-start(bf16[8,7168]{1,0:T(8,128)(2,1)} %param.13) | copy-start | bytes 344068
Sparse Core Ops, SparseCore 0:
  12.2 145.7 all-gather.2
